TPU v7x, 32 devices: a whole 2x2x4 slice. The times are simulated.
32 devices in a mesh: chan: 16 (over z, y, x), facet: 2 (over core).
Axes of the slice: x: 2, y: 2, z: 4, core: 2. Of those that a mesh axis runs over, the one named last changes fastest.
Arguments:
- estimate: float32 [256, 128, 256], P('chan', None, 'facet'), may hold values from -6 to 6
- dirty: float32 [256, 128, 256], P('chan', None, 'facet'), may hold values from -6 to 6
- weights: float32 [256, 128, 256], P('chan', None, 'facet'), may hold values from 0.2 to 1
- margin: int32 [2], replicated, may hold values from 1 to 16, as said below
- blend_table: int32 [2, 160], replicated, may hold values from 1 to 8
- tau_steps: int32 [2], replicated, may hold values from 1 to 4
Outputs:
- updated: float32 [256, 128, 256], P('chan', None, 'facet')
Inputs may be any that keep to these rules, and one draw needn't show every extreme that they name: Some facet has margin exactly 16.
All inputs are finite; a program needn't handle non-finite values.
Results may differ from a plain program's by a relative error of at most 0.00012.
Values sent between devices are 32-bit elements; how exact they have to be, the bound alone decides.
A program may use at most 64 MiB of HBM per device.

v0:
```python
import math

import jax
import jax.numpy as jnp
from jax import lax
from jax.sharding import PartitionSpec as P

OV = 16
NS_STEPS = 2
ITERS = 2


def padded(shard, sides, width):
    for axis, dim in sides:
        size, length = (lax.axis_size(axis), shard.shape[dim])
        up = [(i, (i + 1) % size) for i in range(size - 1)]
        down = [(j, i) for i, j in up]
        last = lax.slice_in_dim(shard, length - width, length, axis=dim)
        initial = lax.slice_in_dim(shard, 0, width, axis=dim)
        before = lax.ppermute(last, axis, up)
        after = lax.ppermute(initial, axis, down)
        shard = jnp.concatenate([before, shard, after], axis=dim)
    return shard


def apply_shrink(gram, columns, tau_value):
    channel_count = gram.shape[0]
    identity = jnp.eye(channel_count, dtype=jnp.float32)
    mean_eigen = jnp.trace(gram) / channel_count + 1e-06
    target = (gram + 0.01 * mean_eigen * identity) / (16.16 * mean_eigen)
    inverse_root = identity
    for newton_step in range(NS_STEPS):
        middle = 1.5 * identity - 0.5 * jnp.dot(
            inverse_root, target, precision=lax.Precision.HIGHEST
        )
        target = jnp.dot(target, middle, precision=lax.Precision.HIGHEST)
        inverse_root = jnp.dot(middle, inverse_root, precision=lax.Precision.HIGHEST)
    factor = 0.1 * tau_value / math.sqrt(1.01)
    kernel = identity - factor * inverse_root
    return jnp.dot(kernel, columns, precision=lax.Precision.HIGHEST)


def shrink_block(block, tau_value):
    columns = block.reshape(block.shape[0], -1)
    partial_value = jnp.dot(columns, columns.T, precision=lax.Precision.HIGHEST)
    gram = lax.psum(partial_value, "chan")
    return apply_shrink(gram, columns, tau_value).reshape(block.shape)


def extend(moved_cube):
    return padded(moved_cube, (("facet", 2),), OV)


def blend_sums(margin, blend_table, facet_id, facet_total, center):
    center_index = jnp.arange(center, dtype=jnp.int32)
    table_float = blend_table.astype(jnp.float32)
    own_part = table_float[facet_id][OV : OV + center]
    before_id = jnp.maximum(facet_id - 1, 0)
    after_id = jnp.minimum(facet_id + 1, facet_total - 1)
    before_slice = jnp.pad(table_float[before_id][center + OV :], (0, center - OV))
    after_slice = jnp.pad(table_float[after_id][:OV], (center - OV, 0))
    before_ok = (facet_id > 0) & (center_index < margin[before_id])
    after_ok = (facet_id < facet_total - 1) & (center_index >= center - margin[after_id])
    return (
        own_part + jnp.where(before_ok, before_slice, 0.0) + jnp.where(after_ok, after_slice, 0.0)
    )


def blend(result, row_weight, denominator, center):
    weighted = result * row_weight
    rims = jnp.concatenate([weighted[:, :, :OV], weighted[:, :, center + OV :]], axis=2)
    received = padded(rims, (("facet", 2),), OV)
    from_before = jnp.pad(received[:, :, :OV], ((0, 0), (0, 0), (0, center - OV)))
    from_after = jnp.pad(
        received[:, :, received.shape[2] - OV :], ((0, 0), (0, 0), (center - OV, 0))
    )
    core_rows = weighted[:, :, OV : OV + center] + from_before + from_after
    return core_rows / denominator


def per_device(estimate, dirty, weights, margin, blend_table, tau_steps):
    facet_id = lax.axis_index("facet")
    facet_total = lax.axis_size("facet")
    center = estimate.shape[2]
    ext_len = center + 2 * OV
    row_index = jnp.arange(ext_len, dtype=jnp.int32)
    own_width = margin[facet_id]
    keep_rows = ((row_index >= OV - own_width) & (row_index < center + OV + own_width)).astype(
        jnp.float32
    )
    row_weight = blend_table[facet_id].astype(jnp.float32) * keep_rows
    denominator = blend_sums(margin, blend_table, facet_id, facet_total, center)
    current, dirty_view, weight_view = (
        lax.all_to_all(estimate, "chan", split_axis=1, concat_axis=0, tiled=True),
        lax.all_to_all(dirty, "chan", split_axis=1, concat_axis=0, tiled=True),
        lax.all_to_all(weights, "chan", split_axis=1, concat_axis=0, tiled=True),
    )
    for iteration in range(ITERS):
        tau_value = tau_steps[iteration].astype(jnp.float32)
        moved_cube = current - weight_view * (current - dirty_view)
        extended = extend(moved_cube) * keep_rows
        result = shrink_block(extended, tau_value)
        current = blend(result, row_weight, denominator, center)
    return lax.all_to_all(current, "chan", split_axis=0, concat_axis=1, tiled=True)


def solution(mesh):
    placed = (
        P("chan", None, "facet"),
        P("chan", None, "facet"),
        P("chan", None, "facet"),
        P(),
        P(),
        P(),
    )
    return jax.shard_map(
        per_device, mesh=mesh, in_specs=placed, out_specs=P("chan", None, "facet"), check_vma=False
    )
```

profile of v0, /device:TPU:0, one launch (start us, length us, event | category | flops | bytes accessed | tf_op | source)
XLA Modules:
  0.0 398.1 jit_solution(12417834899044095266)
XLA Ops:
  6.5 2.8 copy.29
  9.3 8.4 %all-to-all-start = ((f32[16,128,128]{2,0,1:T(8,128)}), f32[16,128,128]{2,0,1:T(8,128)S(1)}, u32[]{:S(2)}, u32[]{:S(2)}) async-start(f32[16,128,128]{2,0,1:T(8,128)} %copy.29), calls=%async_computation | async-start | bytes 2097152 | tf_op jit(solution)/shard_map/all_to_all | solution.py:94
  17.8 1.6 copy.35
  19.4 22.8 %all-to-all-done = f32[16,128,128]{2,0,1:T(8,128)S(1)} async-done(((f32[16,128,128]{2,0,1:T(8,128)}), f32[16,128,128]{2,0,1:T(8,128)S(1)}, u32[]{:S(2)}, u32[]{:S(2)}) %all-to-all-start) | async-done | bytes 1048608 | tf_op jit(solution)/shard_map/all_to_all | solution.py:94
  42.2 5.8 %all-to-all-start.2 = ((f32[16,128,128]{2,0,1:T(8,128)}), f32[16,128,128]{2,0,1:T(8,128)S(1)}, u32[]{:S(2)}, u32[]{:S(2)}) async-start(f32[16,128,128]{2,0,1:T(8,128)} %copy.35), calls=%async_computation.2 | async-start | bytes 2097152 | tf_op jit(solution)/shard_map/all_to_all | solution.py:95
  48.1 1.6 copy.32
  49.7 21.4 %all-to-all-done.2 = f32[16,128,128]{2,0,1:T(8,128)S(1)} async-done(((f32[16,128,128]{2,0,1:T(8,128)}), f32[16,128,128]{2,0,1:T(8,128)S(1)}, u32[]{:S(2)}, u32[]{:S(2)}) %all-to-all-start.2) | async-done | bytes 1048608 | tf_op jit(solution)/shard_map/all_to_all | solution.py:95
  71.0 6.0 %all-to-all-start.1 = ((f32[16,128,128]{2,0,1:T(8,128)}), f32[16,128,128]{2,0,1:T(8,128)S(1)}, u32[]{:S(2)}, u32[]{:S(2)}) async-start(f32[16,128,128]{2,0,1:T(8,128)} %copy.32), calls=%async_computation.1 | async-start | bytes 2097152 | tf_op jit(solution)/shard_map/all_to_all | solution.py:96
  80.5 1.3 copy.31
  81.8 2.6 copy.41
  84.3 1.3 copy.37
  85.6 1.6 copy.39
  87.2 12.7 %all-to-all-done.1 = f32[16,128,128]{2,0,1:T(8,128)S(1)} async-done(((f32[16,128,128]{2,0,1:T(8,128)}), f32[16,128,128]{2,0,1:T(8,128)S(1)}, u32[]{:S(2)}, u32[]{:S(2)}) %all-to-all-start.1) | async-done | bytes 1048608 | tf_op jit(solution)/shard_map/all_to_all | solution.py:96
  99.9 1.3 copy.34
  101.2 1.6 copy.40
  102.7 1.4 multiply_subtract_fusion.1
  104.2 1.3 collective-permute-start
  106.8 1.9 collective-permute-done.1
  108.8 3.1 fusion.4
  112.2 106.9 %all-reduce.9.cloned.1.call-done = f32[256,256]{1,0:T(8,128)} async-done(((f32[256,256]{1,0:T(8,128)}), f32[256,256]{1,0:T(8,128)}) %all-reduce.9.cloned.1.call-update) | async-done | bytes 262160 | tf_op jit(solution)/shard_map/psum | solution.py:46
  219.1 1.6 select_reduce_fusion.1
  221.3 1.3 fusion.17
  226.5 1.3 collective-permute-start.2
  231.1 1.5 multiply_subtract_fusion
  232.6 2.8 collective-permute-start.4
  237.3 1.3 collective-permute-done.5
  238.6 3.1 fusion.7
  242.1 105.5 %all-reduce.11.cloned.1.call-done = f32[256,256]{1,0:T(8,128)} async-done(((f32[256,256]{1,0:T(8,128)}), f32[256,256]{1,0:T(8,128)}) %all-reduce.11.cloned.1.call-update) | async-done | bytes 262160 | tf_op jit(solution)/shard_map/psum | solution.py:46
  347.6 1.7 select_reduce_fusion
  353.9 1.3 collective-permute-start.6
  356.6 1.9 collective-permute-done.7
  359.1 31.1 %all_to_all.72 = f32[256,8,128]{2,1,0:T(8,128)S(1)} all-to-all(f32[256,8,128]{2,1,0:T(8,128)S(1)} %copy.44), channel_id=1, replica_groups=mesh['chan'=16,'facet'=2] {'chan'}, dimensions={0} | all-to-all | bytes 2097152 | tf_op jit(solution)/shard_map/all_to_all | solution.py:104
  (61 shorter events, 18.1 us)
Async XLA Ops:
  9.3 8.5 %copy-start.1 = (f32[16,128,128]{2,1,0:T(8,128)S(1)}, f32[16,128,128]{2,1,0:T(8,128)}, u32[]{:S(2)}) copy-start(f32[16,128,128]{2,1,0:T(8,128)} %param.7) | copy-start | bytes 3145732
  9.3 32.9 %all-to-all-start = ((f32[16,128,128]{2,0,1:T(8,128)}), f32[16,128,128]{2,0,1:T(8,128)S(1)}, u32[]{:S(2)}, u32[]{:S(2)}) async-start(f32[16,128,128]{2,0,1:T(8,128)} %copy.29), calls=%async_computation | async-start | bytes 2097152 | tf_op jit(solution)/shard_map/all_to_all | solution.py:94
  19.4 28.7 %copy-start.2 = (f32[16,128,128]{2,1,0:T(8,128)S(1)}, f32[16,128,128]{2,1,0:T(8,128)}, u32[]{:S(2)}) copy-start(f32[16,128,128]{2,1,0:T(8,128)} %param.8) | copy-start | bytes 3145732
  42.2 28.8 %all-to-all-start.2 = ((f32[16,128,128]{2,0,1:T(8,128)}), f32[16,128,128]{2,0,1:T(8,128)S(1)}, u32[]{:S(2)}, u32[]{:S(2)}) async-start(f32[16,128,128]{2,0,1:T(8,128)} %copy.35), calls=%async_computation.2 | async-start | bytes 2097152 | tf_op jit(solution)/shard_map/all_to_all | solution.py:95
  49.7 27.4 %copy-start.7 = (s32[2]{0:T(128)S(1)}, s32[2]{0:T(128)}, u32[]{:S(2)}) copy-start(s32[2]{0:T(128)} %param.11) | copy-start | bytes 28
  49.7 28.7 %copy-start.6 = (s32[2]{0:T(128)S(1)}, s32[2]{0:T(128)}, u32[]{:S(2)}) copy-start(s32[2]{0:T(128)} %param.9) | copy-start | bytes 28
  49.7 30.7 %copy-start.5 = (s32[2,160]{1,0:T(2,128)S(1)}, s32[2,160]{1,0:T(2,128)}, u32[]{:S(2)}) copy-start(s32[2,160]{1,0:T(2,128)} %param.10) | copy-start | bytes 3844
  71.0 28.8 %all-to-all-start.1 = ((f32[16,128,128]{2,0,1:T(8,128)}), f32[16,128,128]{2,0,1:T(8,128)S(1)}, u32[]{:S(2)}, u32[]{:S(2)}) async-start(f32[16,128,128]{2,0,1:T(8,128)} %copy.32), calls=%async_computation.1 | async-start | bytes 2097152 | tf_op jit(solution)/shard_map/all_to_all | solution.py:96
  77.0 142.1 %all-reduce.9.cloned.1.call-start = ((), (), s32[]{:S(2)}) async-start(), calls=%async_computation.4 | async-start | bytes 524288 | tf_op jit(solution)/shard_map/psum | solution.py:46
  104.2 2.6 collective-permute-start
  105.5 3.2 collective-permute-start.1
  111.8 235.7 %all-reduce.11.cloned.1.call-start = ((), (), s32[]{:S(2)}) async-start(), calls=%async_computation.5 | async-start | bytes 524288 | tf_op jit(solution)/shard_map/psum | solution.py:46
  221.3 1.6 copy-start.4
  225.4 1.1 copy-start
  226.5 4.1 %collective-permute-start.2 = (f32[256,8,16]{0,2,1:T(8,128)S(1)}, f32[256,8,16]{0,2,1:T(8,128)S(1)}, u32[]{:S(2)}, u32[]{:S(2)}) collective-permute-start(f32[256,8,16]{0,2,1:T(8,128)S(1)} %get-tuple-element.7), channel_id=1, source_target_pairs={{0,1},{2,3},{4,5},{6,7},{8,9},{10,11},{12,13},{14,15},{16,17},{18,... | collective-permute-start | bytes 393224 | tf_op jit(solution)/shard_map/ppermute | solution.py:20
  227.8 3.2 collective-permute-start.3
  232.6 4.7 %collective-permute-start.4 = (f32[256,8,16]{0,2,1:T(8,128)S(1)}, f32[256,8,16]{0,2,1:T(8,128)S(1)}, u32[]{:S(2)}, u32[]{:S(2)}) collective-permute-start(f32[256,8,16]{0,2,1:T(8,128)S(1)} %get-tuple-element.9), channel_id=1, source_target_pairs={{0,1},{2,3},{4,5},{6,7},{8,9},{10,11},{12,13},{14,15},{16,17},{18,... | collective-permute-start | bytes 393224 | tf_op jit(solution)/shard_map/ppermute | solution.py:20
  235.4 3.2 collective-permute-start.5
  347.6 3.9 copy-start.3
  353.9 2.6 collective-permute-start.6
  355.2 3.2 collective-permute-start.7
Sparse Core Ops, SparseCore 0:
  112.0 107.0 all-reduce.8
  241.8 105.6 all-reduce.10
where the time goes:
time: 399 us; the launch traced here: 398 us
  waiting for transfers between devices  275 us (69%)
  starting transfers between devices  32.2 us (8%)
  blocking collectives  31.1 us (8%)
  local copies, waits for them, and re-layouts  19.7 us (5%)
  between operations  18.3 us (5%)
  matrix products  14.1 us (4%)
  other arithmetic  7.8 us (2%)
    psum x2, waiting for transfers between devices, shrink_block(): gram = lax.psum(partial_value, 'chan')  212 us
    all_to_all x1, blocking collectives, per_device(): lax.all_to_all(current, 'chan', split_axis=0, concat_axis=1, tiled=True)  31.1 us
    all_to_all x1, waiting for transfers between devices, per_device(): lax.all_to_all(estimate, 'chan', split_axis=1, concat_axis=0, tiled=True)  22.8 us
    all_to_all x1, waiting for transfers between devices, per_device(): lax.all_to_all(dirty, 'chan', split_axis=1, concat_axis=0, tiled=True)  21.4 us
    all_to_all x1, waiting for transfers between devices, per_device(): lax.all_to_all(weights, 'chan', split_axis=1, concat_axis=0, tiled=True)  12.7 us
    all_to_all x1, starting transfers between devices, per_device(): lax.all_to_all(estimate, 'chan', split_axis=1, concat_axis=0, tiled=True)  8.44 us
  transfers between devices with their start and end apart: 13, of which 9 were waited for; matrix products, arithmetic and copies ran while one was open for 3% of the time, Pallas kernels for 0%

commit v1 on v0

v1 whole, which is shorter than its diff:
```python
import functools
import math

import jax
import jax.numpy as jnp
from jax import lax
from jax.experimental import pallas as pl
from jax.experimental.pallas import tpu as pltpu
from jax.sharding import PartitionSpec as P

OV = 16
NS_STEPS = 2
ITERS = 2
MESH = pl.DeviceIdType.MESH
HIGHEST = lax.Precision.HIGHEST
F32 = jnp.float32


def dot(a, b):
    return jnp.dot(a, b, precision=HIGHEST, preferred_element_type=F32)


def dot_nt(a, b):
    return lax.dot_general(
        a, b, (((1,), (1,)), ((), ())), precision=HIGHEST, preferred_element_type=F32
    )


def kernel(
    n, facets, est, dirty, wts, margin, table, tau, out,
    send, recv, cube, gram, kmat, g_part, g_parts, g_sum, g_all,
    halo_out, halo_in, rim, back_out, back_in,
    send_sem, recv_sem, g_send_sem, g_recv_sem, h_send_sem, h_recv_sem,
):
    me = lax.axis_index("chan")
    f = lax.axis_index("facet")
    _, wl, c_loc, rows = out.shape
    total = n * c_loc
    has = (f > 0, f < facets - 1)
    near = (f - 1, f + 1)

    def peers(body):
        def step(s, carry):
            body(lax.rem(me + s, n))
            return carry

        lax.fori_loop(1, n, step, 0)

    def over_columns(body):
        def step(w, carry):
            body(w)
            return carry

        lax.fori_loop(0, wl, step, 0)

    barrier = pltpu.get_barrier_semaphore()
    peers(lambda j: pl.semaphore_signal(barrier, inc=1, device_id={"chan": j}, device_id_type=MESH))
    for s in range(2):
        @pl.when(has[s])
        def _():
            pl.semaphore_signal(
                barrier, inc=1, device_id={"facet": near[s]}, device_id_type=MESH
            )
    sides = lax.min(f, 1) + lax.min(facets - 1 - f, 1)
    pl.semaphore_wait(barrier, n - 1 + sides)

    ext = table.shape[1]
    weights_of = table[...].astype(F32)
    row_of = lax.broadcasted_iota(jnp.int32, (facets, 1), 0)
    e_of = lax.broadcasted_iota(jnp.int32, (ext, rows), 0)
    l_of = lax.broadcasted_iota(jnp.int32, (ext, rows), 1)
    lane = lax.broadcasted_iota(jnp.int32, (1, rows), 1)
    packed = lax.rem(lane, OV)
    packed_of = lax.rem(l_of, OV)

    def facet_row(g, place):
        row = jnp.sum(jnp.where(row_of == g, weights_of, 0.0), axis=0, keepdims=True)
        row = jnp.broadcast_to(row, (8, ext))
        pick = jnp.where(e_of == place, 1.0, 0.0)
        return dot(row, pick)[0:1]

    own_margin = margin[f]
    before_margin = margin[lax.max(f - 1, 0)]
    after_margin = margin[lax.min(f + 1, facets - 1)]
    core_weight = facet_row(f, l_of + OV)
    before_part = facet_row(f - 1, l_of + (rows + OV))
    after_part = facet_row(f + 1, l_of - (rows - OV))
    before_ok = jnp.where((lane < before_margin) & (f > 0), 1.0, 0.0)
    after_ok = jnp.where((lane >= rows - after_margin) & (f < facets - 1), 1.0, 0.0)
    inverse = 1.0 / (core_weight + before_part * before_ok + after_part * after_ok)
    used = jnp.where(lane < wl * OV, 1.0, 0.0)
    rim_mask = (
        jnp.where(packed >= OV - own_margin, 1.0, 0.0) * used,
        jnp.where(packed < own_margin, 1.0, 0.0) * used,
    )
    rim_weight = (
        facet_row(f, packed_of) * rim_mask[0],
        facet_row(f, packed_of + (rows + OV)) * rim_mask[1],
    )

    def block_copy(k, j, landing):
        return pltpu.make_async_remote_copy(
            src_ref=send.at[k, j],
            dst_ref=landing,
            send_sem=send_sem.at[k, j],
            recv_sem=recv_sem.at[k, me],
            device_id={"chan": j},
            device_id_type=MESH,
        )

    def block_wait(k, j, landing):
        pltpu.make_async_remote_copy(
            src_ref=send.at[k, j],
            dst_ref=landing,
            send_sem=send_sem.at[k, j],
            recv_sem=recv_sem.at[k, j],
            device_id={"chan": j},
            device_id_type=MESH,
        ).wait_recv()

    def turned(value):
        return jnp.swapaxes(value, 0, 1)

    def send_moved(j):
        value = est[:, j]
        send[0, j] = turned(value - wts[:, j] * (value - dirty[:, j]))
        block_copy(0, j, recv.at[0, me]).start()

    def send_weights(j):
        send[1, j] = turned(wts[:, j])
        block_copy(1, j, recv.at[1, me]).start()

    peers(send_moved)
    peers(send_weights)

    def stage_dirty(j):
        send[2, j] = turned(dirty[:, j])

    peers(stage_dirty)
    mine = est[:, me]
    recv[0, me] = turned(mine - wts[:, me] * (mine - dirty[:, me]))
    recv[1, me] = turned(wts[:, me])
    recv[2, me] = turned(dirty[:, me])

    def send_dirty(first, last):
        def step(s, carry):
            block_copy(2, lax.rem(me + s, n), recv.at[2, me]).start()
            return carry

        lax.fori_loop(first, last, step, 0)

    half = n // 2

    peers(lambda j: block_wait(0, j, recv.at[0, j]))

    def matrix(k, w):
        return recv[k, :, w].reshape(total, rows)

    def side_copy(it, what, src, dst, s, there):
        return pltpu.make_async_remote_copy(
            src_ref=src.at[it, s],
            dst_ref=dst.at[it, there],
            send_sem=h_send_sem.at[it, what, s],
            recv_sem=h_recv_sem.at[it, what, there],
            device_id={"facet": near[s]},
            device_id_type=MESH,
        )

    eye = jnp.where(
        lax.broadcasted_iota(jnp.int32, (total, total), 0)
        == lax.broadcasted_iota(jnp.int32, (total, total), 1),
        1.0,
        0.0,
    )

    for it in range(ITERS):
        for s in range(2):
            @pl.when(has[s])
            def _():
                low = 0 if s == 0 else rows - OV
                block = jnp.zeros((total, rows), F32)
                for w in range(wl):
                    rolled = pltpu.roll(matrix(0, w), (w * OV - low) % rows, 1)
                    block = jnp.where(lane // OV == w, rolled, block)
                halo_out[it, s] = block
                side_copy(it, 0, halo_out, halo_in, s, 1 - s).start()

        gram[...] = jnp.zeros((total, total), F32)

        def add_gram(w):
            m = matrix(0, w)
            gram[...] += dot_nt(m, m)

        over_columns(add_gram)
        for s in range(2):
            @pl.when(has[s])
            def _():
                side_copy(it, 0, halo_out, halo_in, s, s).wait_recv()
                m = halo_in[it, s] * rim_mask[s]
                rim[s] = m
                gram[...] += dot_nt(m, m)

        g_part[it] = gram[...].reshape(n, c_loc, total)

        def g_copy(what, src, dst, j, sem_at):
            return pltpu.make_async_remote_copy(
                src_ref=src,
                dst_ref=dst,
                send_sem=g_send_sem.at[it, what, j],
                recv_sem=g_recv_sem.at[it, what, sem_at],
                device_id={"chan": j},
                device_id_type=MESH,
            )

        peers(lambda j: g_copy(0, g_part.at[it, j], g_parts.at[it, me], j, me).start())
        g_parts[it, me] = g_part[it, me]
        if it == 0:
            send_dirty(1, half)
        peers(lambda j: g_copy(0, g_part.at[it, j], g_parts.at[it, j], j, j).wait_recv())
        g_sum[it] = jnp.sum(g_parts[it], axis=0)
        peers(lambda j: g_copy(1, g_sum.at[it], g_all.at[it, me], j, me).start())
        g_all[it, me] = g_sum[it]
        if it == 0:
            send_dirty(half, n)
        peers(lambda j: g_copy(1, g_sum.at[it], g_all.at[it, j], j, j).wait_recv())

        full = g_all[it].reshape(total, total)
        mean = jnp.sum(full * eye) / total + 1e-06
        target = (full + (0.01 * mean) * eye) / (16.16 * mean)
        middle = 1.5 * eye - 0.5 * target
        root = middle
        for _step in range(NS_STEPS - 1):
            target = dot(target, middle)
            middle = 1.5 * eye - 0.5 * dot(root, target)
            root = dot(middle, root)
        factor = (0.1 / math.sqrt(1.01)) * tau[it].astype(F32)
        kmat[...] = eye - factor * root

        for s in range(2):
            @pl.when(has[s])
            def _():
                back_out[it, s] = dot(kmat[...], rim[s]) * rim_weight[s]
                side_copy(it, 1, back_out, back_in, s, 1 - s).start()

        def shrink(w):
            value = dot(kmat[...], matrix(0, w)) * (core_weight * inverse)
            cube[:, w] = value.reshape(n, c_loc, rows)

        over_columns(shrink)
        for s in range(2):
            @pl.when(has[s])
            def _():
                side_copy(it, 1, back_out, back_in, s, s).wait_recv()
                low = 0 if s == 0 else rows - OV
                inside = (lane >= low) & (lane < low + OV)
                extra = back_in[it, s]
                for w in range(wl):
                    rolled = pltpu.roll(extra, (low - w * OV) % rows, 1)
                    piece = jnp.where(inside, rolled * inverse, 0.0)
                    cube[:, w] += piece.reshape(n, c_loc, rows)

        if it < ITERS - 1:
            if it == 0:
                peers(lambda j: block_wait(1, j, recv.at[1, j]))
                peers(lambda j: block_wait(2, j, recv.at[2, j]))

            def move(w):
                value = cube[:, w]
                recv[0, :, w] = value - recv[1, :, w] * (value - recv[2, :, w])

            over_columns(move)

    def final_copy(j, landing, sem_at):
        return pltpu.make_async_remote_copy(
            src_ref=cube.at[j],
            dst_ref=landing,
            send_sem=send_sem.at[3, j],
            recv_sem=recv_sem.at[3, sem_at],
            device_id={"chan": j},
            device_id_type=MESH,
        )

    peers(lambda j: final_copy(j, out.at[me], me).start())
    out[me] = cube[me]

    def drain(j):
        for k in range(3):
            block_copy(k, j, recv.at[k, me]).wait_send()
        for it in range(ITERS):
            for what in range(2):
                src = g_part.at[it, j] if what == 0 else g_sum.at[it]
                dst = g_parts.at[it, me] if what == 0 else g_all.at[it, me]
                pltpu.make_async_remote_copy(
                    src_ref=src,
                    dst_ref=dst,
                    send_sem=g_send_sem.at[it, what, j],
                    recv_sem=g_recv_sem.at[it, what, me],
                    device_id={"chan": j},
                    device_id_type=MESH,
                ).wait_send()

    peers(drain)
    for s in range(2):
        @pl.when(has[s])
        def _():
            for it in range(ITERS):
                side_copy(it, 0, halo_out, halo_in, s, 1 - s).wait_send()
                side_copy(it, 1, back_out, back_in, s, 1 - s).wait_send()
    peers(lambda j: final_copy(j, out.at[j], j).wait_recv())
    peers(lambda j: final_copy(j, out.at[me], me).wait_send())


def per_device(n, facets, estimate, dirty, weights, margin, blend_table, tau_steps):
    c_loc, width, rows = estimate.shape
    wl = width // n
    total = n * c_loc
    cut = lambda a: a.reshape(c_loc, n, wl, rows)
    vmem = pl.BlockSpec(memory_space=pltpu.VMEM)
    smem = pl.BlockSpec(memory_space=pltpu.SMEM)
    dma = pltpu.SemaphoreType.DMA
    result = pl.pallas_call(
        functools.partial(kernel, n, facets),
        out_shape=jax.ShapeDtypeStruct((n, wl, c_loc, rows), F32),
        in_specs=[vmem, vmem, vmem, smem, vmem, smem],
        out_specs=vmem,
        scratch_shapes=[
            pltpu.VMEM((3, n, wl, c_loc, rows), F32),
            pltpu.VMEM((3, n, wl, c_loc, rows), F32),
            pltpu.VMEM((n, wl, c_loc, rows), F32),
            pltpu.VMEM((total, total), F32),
            pltpu.VMEM((total, total), F32),
            pltpu.VMEM((ITERS, n, c_loc, total), F32),
            pltpu.VMEM((ITERS, n, c_loc, total), F32),
            pltpu.VMEM((ITERS, c_loc, total), F32),
            pltpu.VMEM((ITERS, n, c_loc, total), F32),
            pltpu.VMEM((ITERS, 2, total, rows), F32),
            pltpu.VMEM((ITERS, 2, total, rows), F32),
            pltpu.VMEM((2, total, rows), F32),
            pltpu.VMEM((ITERS, 2, total, rows), F32),
            pltpu.VMEM((ITERS, 2, total, rows), F32),
            dma((4, n)),
            dma((4, n)),
            dma((ITERS, 2, n)),
            dma((ITERS, 2, n)),
            dma((ITERS, 2, 2)),
            dma((ITERS, 2, 2)),
        ],
        compiler_params=pltpu.CompilerParams(
            collective_id=0, has_side_effects=True, vmem_limit_bytes=48 * 1024 * 1024
        ),
        cost_estimate=pl.CostEstimate(
            flops=ITERS * 4 * total * total * wl * (rows + 2 * OV),
            bytes_accessed=16 * c_loc * width * rows,
            transcendentals=0,
        ),
        name="denoise",
    )(cut(estimate), cut(dirty), cut(weights), margin, blend_table, tau_steps)
    return result.transpose(2, 0, 1, 3).reshape(c_loc, width, rows)


def solution(mesh):
    n, facets = mesh.shape["chan"], mesh.shape["facet"]
    cube = P("chan", None, "facet")
    return jax.shard_map(
        functools.partial(per_device, n, facets),
        mesh=mesh,
        in_specs=(cube, cube, cube, P(), P(), P()),
        out_specs=cube,
        check_vma=False,
    )
```

time: 399 us -> 148 us (0.37)
  the two profiles are of different devices: /device:TPU:0 before, /device:TPU:12 now
where the time goes in v1:
time: 148 us
  Pallas kernels  142 us (96%)
  local copies, waits for them, and re-layouts  5.65 us (4%)
    pallas_call x1, Pallas kernels, per_device(): pl.pallas_call(functools.partial(kernel, n, facets), out_shape=jax.ShapeD...  142 us
    unnamed x12, local copies, waits for them, and re-layouts  4.36 us

profile of v1, /device:TPU:12, one launch (start us, length us, event | category | flops | bytes accessed | tf_op | source)
XLA Modules:
  0.0 147.6 jit_solution(874809873228534011)
XLA Ops:
  0.0 0.0 copy-start.3
  0.0 0.0 copy-start.4
  0.0 0.0 copy-start.5
  0.0 0.7 copy-done.3
  0.7 0.0 copy-done.4
  0.7 0.0 copy-done.5
  0.7 0.0 copy-start
  0.7 1.2 copy-done
  1.9 0.0 copy-start.1
  1.9 1.2 copy-done.1
  3.1 0.0 copy-start.2
  3.1 1.2 copy-done.2
  4.4 141.9 %denoise.1 = f32[16,8,16,128]{3,2,1,0:T(8,128)S(1)} custom-call(f32[16,16,8,128]{3,2,1,0:T(8,128)S(1)} %bitcast.7, f32[16,16,8,128]{3,2,1,0:T(8,128)S(1)} %bitcast.8, f32[16,16,8,128]{3,2,1,0:T(8,128)S(1)} %bitcast.9, s32[2]{0:T(128)S(1)} %copy-done.4, s32[2,160]{1,0:T(2,128)S(1)} %copy-done.3, s32[2]{0:T(128)S(1)} %copy-done.5), custom_call_target="tpu_custom_call" | custom-call | flops 671088640 | bytes 4194304 | tf_op jit(solution)/shard_map/denoise/pallas_call | solution.py:321
  146.3 1.3 copy.7
Async XLA Ops:
  0.0 0.7 copy-start.3
  0.0 0.7 copy-start.4
  0.0 0.7 copy-start.5
  0.7 1.2 copy-start
  1.9 1.2 copy-start.1
  3.1 1.2 copy-start.2

commit v2 on v1

v2 whole, which is shorter than its diff:
```python
import functools
import math

import jax
import jax.numpy as jnp
from jax import lax
from jax.experimental import pallas as pl
from jax.experimental.pallas import tpu as pltpu
from jax.sharding import PartitionSpec as P

OV = 16
NS_STEPS = 2
ITERS = 2
MESH = pl.DeviceIdType.MESH
F32 = jnp.float32
BF16 = jnp.bfloat16


def dot(a, b):
    return jnp.dot(a, b, preferred_element_type=F32)


def dot_nt(a, b):
    return lax.dot_general(a, b, (((1,), (1,)), ((), ())), preferred_element_type=F32)


def split(value):
    high = value.astype(BF16)
    return high, (value - high.astype(F32)).astype(BF16)


def dot_split(a, b):
    return dot(a[0], b[0]) + (dot(a[0], b[1]) + dot(a[1], b[0]))


def kernel(
    n, facets, est_hbm, dirty_hbm, wts_hbm, margin, table, tau, out,
    est, dirty, wts, send, recv, cube, high, low, gram, g_part, g_parts, g_sum, g_all,
    halo_out, halo_in, rim, back_out, back_in,
    in_sem, send_sem, recv_sem, g_send_sem, g_recv_sem, h_send_sem, h_recv_sem,
):
    me = lax.axis_index("chan")
    f = lax.axis_index("facet")
    _, wl, c_loc, rows = out.shape
    total = n * c_loc
    has = (f > 0, f < facets - 1)
    near = (f - 1, f + 1)
    half = n // 2
    upper, place = me // half, lax.rem(me, half)

    def peers(body):
        def step(t, carry):
            other = lax.rem(place + t, half)
            body((1 - upper) * half + other)
            body(upper * half + other)
            return carry

        body((1 - upper) * half + place)
        lax.fori_loop(1, half, step, 0)

    loads = [
        pltpu.make_async_copy(src, dst, in_sem.at[i])
        for i, (src, dst) in enumerate(((est_hbm, est), (dirty_hbm, dirty), (wts_hbm, wts)))
    ]
    for load in loads:
        load.start()

    barrier = pltpu.get_barrier_semaphore()
    peers(lambda j: pl.semaphore_signal(barrier, inc=1, device_id={"chan": j}, device_id_type=MESH))
    for s in range(2):
        @pl.when(has[s])
        def _():
            pl.semaphore_signal(
                barrier, inc=1, device_id={"facet": near[s]}, device_id_type=MESH
            )
    sides = lax.min(f, 1) + lax.min(facets - 1 - f, 1)
    pl.semaphore_wait(barrier, n - 1 + sides)
    for load in loads:
        load.wait()

    cut = wl // 2
    sets = ((0, 0, wl), (1, 0, wl), (2, 0, cut), (2, cut, wl - cut))

    def block_copy(q, j, origin, sem_at):
        k, first, count = sets[q]
        return pltpu.make_async_remote_copy(
            src_ref=send.at[k, j, pl.ds(first, count)],
            dst_ref=recv.at[k, origin, pl.ds(first, count)],
            send_sem=send_sem.at[q, j],
            recv_sem=recv_sem.at[q, sem_at],
            device_id={"chan": j},
            device_id_type=MESH,
        )

    def block_send(q):
        peers(lambda j: block_copy(q, j, me, me).start())

    def block_wait(q):
        peers(lambda j: block_copy(q, j, j, j).wait_recv())

    def turned(value):
        return jnp.swapaxes(value, 0, 1)

    def send_moved(j):
        value = est[:, j]
        send[0, j] = turned(value - wts[:, j] * (value - dirty[:, j]))
        block_copy(0, j, me, me).start()

    def send_weights(j):
        send[1, j] = turned(wts[:, j])
        block_copy(1, j, me, me).start()

    def stage_dirty(j):
        send[2, j] = turned(dirty[:, j])

    peers(send_moved)
    peers(send_weights)
    peers(stage_dirty)
    mine = est[:, me]
    recv[0, me] = turned(mine - wts[:, me] * (mine - dirty[:, me]))
    recv[1, me] = turned(wts[:, me])
    recv[2, me] = turned(dirty[:, me])

    ext = table.shape[1]
    weights_of = table[...].astype(F32)
    row_of = lax.broadcasted_iota(jnp.int32, (facets, 1), 0)
    e_of = lax.broadcasted_iota(jnp.int32, (ext, rows), 0)
    l_of = lax.broadcasted_iota(jnp.int32, (ext, rows), 1)
    lane = lax.broadcasted_iota(jnp.int32, (1, rows), 1)
    packed = lax.rem(lane, OV)
    packed_of = lax.rem(l_of, OV)

    def facet_row(g, where):
        row = jnp.sum(jnp.where(row_of == g, weights_of, 0.0), axis=0, keepdims=True)
        row = jnp.broadcast_to(row, (16, ext)).astype(BF16)
        pick = jnp.where(e_of == where, 1.0, 0.0).astype(BF16)
        return dot(row, pick)[0:1]

    own_margin = margin[f]
    before_margin = margin[lax.max(f - 1, 0)]
    after_margin = margin[lax.min(f + 1, facets - 1)]
    core_weight = facet_row(f, l_of + OV)
    before_part = facet_row(f - 1, l_of + (rows + OV))
    after_part = facet_row(f + 1, l_of - (rows - OV))
    before_ok = jnp.where((lane < before_margin) & (f > 0), 1.0, 0.0)
    after_ok = jnp.where((lane >= rows - after_margin) & (f < facets - 1), 1.0, 0.0)
    inverse = 1.0 / (core_weight + before_part * before_ok + after_part * after_ok)
    used = jnp.where(lane < wl * OV, 1.0, 0.0)
    rim_mask = (
        jnp.where(packed >= OV - own_margin, 1.0, 0.0) * used,
        jnp.where(packed < own_margin, 1.0, 0.0) * used,
    )
    rim_weight = (
        facet_row(f, packed_of) * rim_mask[0],
        facet_row(f, packed_of + (rows + OV)) * rim_mask[1],
    )
    eye = jnp.where(
        lax.broadcasted_iota(jnp.int32, (total, total), 0)
        == lax.broadcasted_iota(jnp.int32, (total, total), 1),
        1.0,
        0.0,
    )

    def block(first, count=1):
        return slice(first * rows, (first + count) * rows)

    def matrix(k, w):
        return recv[k, :, w].reshape(total, rows)

    def put(at, value):
        high[:, block(at)], low[:, block(at)] = split(value)

    def add_gram(first, count, fresh):
        h, l = high[:, block(first, count)], low[:, block(first, count)]
        same, cross = dot_nt(h, h), dot_nt(h, l)
        if fresh:
            gram[0], gram[1] = same, cross
        else:
            gram[0] += same
            gram[1] += cross

    high[:, block(wl, 2)] = jnp.zeros((total, 2 * rows), BF16)
    low[:, block(wl, 2)] = jnp.zeros((total, 2 * rows), BF16)

    def side_copy(it, what, src, dst, s, there):
        return pltpu.make_async_remote_copy(
            src_ref=src.at[it, s],
            dst_ref=dst.at[it, there],
            send_sem=h_send_sem.at[it, what, s],
            recv_sem=h_recv_sem.at[it, what, there],
            device_id={"facet": near[s]},
            device_id_type=MESH,
        )

    def scatter_copy(it, j, origin, sem_at):
        return pltpu.make_async_remote_copy(
            src_ref=g_part.at[it, j],
            dst_ref=g_parts.at[it, origin],
            send_sem=g_send_sem.at[it, 0, j],
            recv_sem=g_recv_sem.at[it, 0, sem_at],
            device_id={"chan": j},
            device_id_type=MESH,
        )

    def gather_copy(it, j, origin, sem_at):
        return pltpu.make_async_remote_copy(
            src_ref=g_sum.at[it],
            dst_ref=g_all.at[it, origin],
            send_sem=g_send_sem.at[it, 1, j],
            recv_sem=g_recv_sem.at[it, 1, sem_at],
            device_id={"chan": j},
            device_id_type=MESH,
        )

    def final_copy(j, landing, sem_at):
        return pltpu.make_async_remote_copy(
            src_ref=cube.at[j],
            dst_ref=landing,
            send_sem=send_sem.at[4, j],
            recv_sem=recv_sem.at[4, sem_at],
            device_id={"chan": j},
            device_id_type=MESH,
        )

    block_wait(0)
    hc = total // 2
    for it in range(ITERS):
        for s in range(2):
            @pl.when(has[s])
            def _():
                start = 0 if s == 0 else rows - OV
                rows_out = jnp.zeros((total, rows), F32)
                for w in range(wl):
                    rolled = pltpu.roll(matrix(0, w), (w * OV - start) % rows, 1)
                    rows_out = jnp.where(lane // OV == w, rolled, rows_out)
                halo_out[it, s] = rows_out
                side_copy(it, 0, halo_out, halo_in, s, 1 - s).start()

        if it == 0:
            for w in range(wl):
                put(w, matrix(0, w))
            add_gram(0, wl, True)
        else:
            add_gram(cut, wl - cut, False)
        for s in range(2):
            @pl.when(has[s])
            def _():
                side_copy(it, 0, halo_out, halo_in, s, s).wait_recv()
                m = halo_in[it, s] * rim_mask[s]
                rim[s] = m
                put(wl + s, m)
        add_gram(wl, 2, False)

        cross = gram[1]
        whole = gram[0] + (cross + cross.T)
        blocks = jnp.concatenate([whole[:hc, :hc], whole[hc:, :hc], whole[hc:, hc:]], axis=0)
        g_part[it] = blocks.reshape(g_part.shape[1:])
        peers(lambda j: scatter_copy(it, j, me, me).start())
        g_parts[it, me] = g_part[it, me]
        if it == 0:
            block_send(2)
        peers(lambda j: scatter_copy(it, j, j, j).wait_recv())
        g_sum[it] = jnp.sum(g_parts[it], axis=0)
        peers(lambda j: gather_copy(it, j, me, me).start())
        g_all[it, me] = g_sum[it]
        if it == 0:
            block_send(3)
        peers(lambda j: gather_copy(it, j, j, j).wait_recv())

        blocks = g_all[it].reshape(3 * hc, hc)
        top, corner, end = blocks[:hc], blocks[hc : 2 * hc], blocks[2 * hc :]
        full = jnp.concatenate(
            [jnp.concatenate([top, corner.T], axis=1), jnp.concatenate([corner, end], axis=1)],
            axis=0,
        )
        mean = jnp.sum(full * eye) / total + 1e-06
        target = (full + (0.01 * mean) * eye) / (16.16 * mean)
        middle = 1.5 * eye - 0.5 * target
        root = middle
        for _step in range(NS_STEPS - 1):
            target = dot_split(split(target), split(middle))
            middle = 1.5 * eye - 0.5 * dot_split(split(root), split(target))
            root = dot_split(split(middle), split(root))
        factor = (0.1 / math.sqrt(1.01)) * tau[it].astype(F32)
        taken = split(factor * root)

        def product(first, count):
            at = block(first, count)
            return dot_split(taken, (high[:, at], low[:, at]))

        for s in range(2):
            @pl.when(has[s])
            def _():
                back_out[it, s] = (rim[s] - product(wl + s, 1)) * rim_weight[s]
                side_copy(it, 1, back_out, back_in, s, 1 - s).start()

        scale = core_weight * inverse
        for w in range(0, wl, 2):
            less = product(w, 2)
            for i in range(2):
                value = (matrix(0, w + i) - less[:, block(i)]) * scale
                cube[:, w + i] = value.reshape(n, c_loc, rows)
        for s in range(2):
            @pl.when(has[s])
            def _():
                side_copy(it, 1, back_out, back_in, s, s).wait_recv()
                start = 0 if s == 0 else rows - OV
                inside = (lane >= start) & (lane < start + OV)
                extra = back_in[it, s]
                for w in range(wl):
                    rolled = pltpu.roll(extra, (start - w * OV) % rows, 1)
                    piece = jnp.where(inside, rolled * inverse, 0.0)
                    cube[:, w] += piece.reshape(n, c_loc, rows)

        if it < ITERS - 1:
            def move(w):
                value = cube[:, w]
                value = value - recv[1, :, w] * (value - recv[2, :, w])
                recv[0, :, w] = value
                put(w, value.reshape(total, rows))

            if it == 0:
                block_wait(1)
                block_wait(2)
            for w in range(cut):
                move(w)
            add_gram(0, cut, True)
            if it == 0:
                block_wait(3)
            for w in range(cut, wl):
                move(w)

    peers(lambda j: final_copy(j, out.at[me], me).start())
    out[me] = cube[me]

    def drain(j):
        for q in range(len(sets)):
            block_copy(q, j, me, me).wait_send()
        for it in range(ITERS):
            scatter_copy(it, j, me, me).wait_send()
            gather_copy(it, j, me, me).wait_send()

    peers(drain)
    for s in range(2):
        @pl.when(has[s])
        def _():
            for it in range(ITERS):
                side_copy(it, 0, halo_out, halo_in, s, 1 - s).wait_send()
                side_copy(it, 1, back_out, back_in, s, 1 - s).wait_send()
    peers(lambda j: final_copy(j, out.at[j], j).wait_recv())
    peers(lambda j: final_copy(j, out.at[me], me).wait_send())


def per_device(n, facets, estimate, dirty, weights, margin, blend_table, tau_steps):
    c_loc, width, rows = estimate.shape
    wl = width // n
    total = n * c_loc
    piece = 3 * total // (2 * n)
    cut = lambda a: a.reshape(c_loc, n, wl, rows)
    vmem = pl.BlockSpec(memory_space=pltpu.VMEM)
    hbm = pl.BlockSpec(memory_space=pltpu.HBM)
    smem = pl.BlockSpec(memory_space=pltpu.SMEM)
    dma = pltpu.SemaphoreType.DMA
    result = pl.pallas_call(
        functools.partial(kernel, n, facets),
        out_shape=jax.ShapeDtypeStruct((n, wl, c_loc, rows), F32),
        in_specs=[hbm, hbm, hbm, smem, vmem, smem],
        out_specs=vmem,
        scratch_shapes=[
            pltpu.VMEM((c_loc, n, wl, rows), F32),
            pltpu.VMEM((c_loc, n, wl, rows), F32),
            pltpu.VMEM((c_loc, n, wl, rows), F32),
            pltpu.VMEM((3, n, wl, c_loc, rows), F32),
            pltpu.VMEM((3, n, wl, c_loc, rows), F32),
            pltpu.VMEM((n, wl, c_loc, rows), F32),
            pltpu.VMEM((total, (wl + 2) * rows), BF16),
            pltpu.VMEM((total, (wl + 2) * rows), BF16),
            pltpu.VMEM((2, total, total), F32),
            pltpu.VMEM((ITERS, n, piece, total // 2), F32),
            pltpu.VMEM((ITERS, n, piece, total // 2), F32),
            pltpu.VMEM((ITERS, piece, total // 2), F32),
            pltpu.VMEM((ITERS, n, piece, total // 2), F32),
            pltpu.VMEM((ITERS, 2, total, rows), F32),
            pltpu.VMEM((ITERS, 2, total, rows), F32),
            pltpu.VMEM((2, total, rows), F32),
            pltpu.VMEM((ITERS, 2, total, rows), F32),
            pltpu.VMEM((ITERS, 2, total, rows), F32),
            dma((3,)),
            dma((5, n)),
            dma((5, n)),
            dma((ITERS, 2, n)),
            dma((ITERS, 2, n)),
            dma((ITERS, 2, 2)),
            dma((ITERS, 2, 2)),
        ],
        compiler_params=pltpu.CompilerParams(
            collective_id=0, has_side_effects=True, vmem_limit_bytes=48 * 1024 * 1024
        ),
        cost_estimate=pl.CostEstimate(
            flops=ITERS * 4 * total * total * wl * (rows + 2 * OV),
            bytes_accessed=16 * c_loc * width * rows,
            transcendentals=0,
        ),
        name="denoise",
    )(cut(estimate), cut(dirty), cut(weights), margin, blend_table, tau_steps)
    return result.transpose(2, 0, 1, 3).reshape(c_loc, width, rows)


def solution(mesh):
    n, facets = mesh.shape["chan"], mesh.shape["facet"]
    cube = P("chan", None, "facet")
    return jax.shard_map(
        functools.partial(per_device, n, facets),
        mesh=mesh,
        in_specs=(cube, cube, cube, P(), P(), P()),
        out_specs=cube,
        check_vma=False,
    )
```

time: 148 us -> 137 us (0.926)
  the two profiles are of different devices: /device:TPU:12 before, /device:TPU:0 now
where the time goes in v2:
time: 137 us
  Pallas kernels  131 us (96%)
  local copies, waits for them, and re-layouts  5.65 us (4%)
    pallas_call x1, Pallas kernels, per_device(): pl.pallas_call(functools.partial(kernel, n, facets), out_shape=jax.ShapeD...  131 us
    unnamed x12, local copies, waits for them, and re-layouts  4.36 us

profile of v2, /device:TPU:0, one launch (start us, length us, event | category | flops | bytes accessed | tf_op | source)
XLA Modules:
  0.0 136.8 jit_solution(4699404808927926263)
XLA Ops:
  0.0 0.0 copy-start.3
  0.0 0.0 copy-start.4
  0.0 0.0 copy-start.5
  0.0 0.7 copy-done.3
  0.7 0.0 copy-done.4
  0.7 0.0 copy-done.5
  0.7 0.0 copy-start
  0.7 1.2 copy-done
  1.9 0.0 copy-start.1
  1.9 1.2 copy-done.1
  3.1 0.0 copy-start.2
  3.1 1.2 copy-done.2
  4.4 131.1 %denoise.1 = f32[16,8,16,128]{3,2,1,0:T(8,128)S(1)} custom-call(f32[16,16,8,128]{3,2,1,0:T(8,128)S(1)} %bitcast.7, f32[16,16,8,128]{3,2,1,0:T(8,128)S(1)} %bitcast.8, f32[16,16,8,128]{3,2,1,0:T(8,128)S(1)} %bitcast.9, s32[2]{0:T(128)S(1)} %copy-done.4, s32[2,160]{1,0:T(2,128)S(1)} %copy-done.3, s32[2]{0:T(128)S(1)} %copy-done.5), custom_call_target="tpu_custom_call" | custom-call | flops 671088640 | bytes 4194304 | tf_op jit(solution)/shard_map/denoise/pallas_call | solution.py:364
  135.5 1.3 copy.7
Async XLA Ops:
  0.0 0.7 copy-start.3
  0.0 0.7 copy-start.4
  0.0 0.7 copy-start.5
  0.7 1.2 copy-start
  1.9 1.2 copy-start.1
  3.1 1.2 copy-start.2

commit v3 on v2

--- a/solution.py
+++ b/solution.py
@@ -35,9 +35,9 @@
 
 def kernel(
     n, facets, est_hbm, dirty_hbm, wts_hbm, margin, table, tau, out,
-    est, dirty, wts, send, recv, cube, high, low, gram, g_part, g_parts, g_sum, g_all,
+    est, dirty, wts, send, recv, cube, high, low, gram, g_part, g_parts, g_half, g_pair, g_sum, g_all,
     halo_out, halo_in, rim, back_out, back_in,
-    in_sem, send_sem, recv_sem, g_send_sem, g_recv_sem, h_send_sem, h_recv_sem,
+    in_sem, send_sem, recv_sem, g_send_sem, g_recv_sem, p_send_sem, p_recv_sem, h_send_sem, h_recv_sem,
 ):
     me = lax.axis_index("chan")
     f = lax.axis_index("facet")
@@ -47,6 +47,7 @@
     near = (f - 1, f + 1)
     half = n // 2
     upper, place = me // half, lax.rem(me, half)
+    mirror = (1 - upper) * half + place
 
     def peers(body):
         def step(t, carry):
@@ -55,7 +56,14 @@
             body(upper * half + other)
             return carry
 
-        body((1 - upper) * half + place)
+        body(mirror)
+        lax.fori_loop(1, half, step, 0)
+
+    def inside_half(body):
+        def step(t, carry):
+            body(lax.rem(place + t, half))
+            return carry
+
         lax.fori_loop(1, half, step, 0)
 
     loads = [
@@ -79,7 +87,8 @@
         load.wait()
 
     cut = wl // 2
-    sets = ((0, 0, wl), (1, 0, wl), (2, 0, cut), (2, cut, wl - cut))
+    halves = ((0, cut), (cut, wl - cut))
+    sets = ((0, 0, wl),) + tuple((k, *h) for k in (1, 2) for h in halves)
 
     def block_copy(q, j, origin, sem_at):
         k, first, count = sets[q]
@@ -192,32 +201,43 @@
             device_id_type=MESH,
         )
 
-    def scatter_copy(it, j, origin, sem_at):
-        return pltpu.make_async_remote_copy(
-            src_ref=g_part.at[it, j],
+    def scatter_copy(it, p, origin, sem_at):
+        return pltpu.make_async_remote_copy(
+            src_ref=g_part.at[it, p],
             dst_ref=g_parts.at[it, origin],
-            send_sem=g_send_sem.at[it, 0, j],
+            send_sem=g_send_sem.at[it, 0, p],
             recv_sem=g_recv_sem.at[it, 0, sem_at],
-            device_id={"chan": j},
-            device_id_type=MESH,
-        )
-
-    def gather_copy(it, j, origin, sem_at):
+            device_id={"chan": upper * half + p},
+            device_id_type=MESH,
+        )
+
+    def gather_copy(it, p, origin, sem_at):
         return pltpu.make_async_remote_copy(
             src_ref=g_sum.at[it],
             dst_ref=g_all.at[it, origin],
-            send_sem=g_send_sem.at[it, 1, j],
+            send_sem=g_send_sem.at[it, 1, p],
             recv_sem=g_recv_sem.at[it, 1, sem_at],
-            device_id={"chan": j},
-            device_id_type=MESH,
-        )
-
-    def final_copy(j, landing, sem_at):
-        return pltpu.make_async_remote_copy(
-            src_ref=cube.at[j],
-            dst_ref=landing,
-            send_sem=send_sem.at[4, j],
-            recv_sem=recv_sem.at[4, sem_at],
+            device_id={"chan": upper * half + p},
+            device_id_type=MESH,
+        )
+
+    def pair_copy(it):
+        return pltpu.make_async_remote_copy(
+            src_ref=g_half.at[it],
+            dst_ref=g_pair.at[it],
+            send_sem=p_send_sem.at[it],
+            recv_sem=p_recv_sem.at[it],
+            device_id={"chan": mirror},
+            device_id_type=MESH,
+        )
+
+    def final_copy(h, j, origin, sem_at):
+        first, count = halves[h]
+        return pltpu.make_async_remote_copy(
+            src_ref=cube.at[j, pl.ds(first, count)],
+            dst_ref=out.at[origin, pl.ds(first, count)],
+            send_sem=send_sem.at[5 + h, j],
+            recv_sem=recv_sem.at[5 + h, sem_at],
             device_id={"chan": j},
             device_id_type=MESH,
         )
@@ -255,17 +275,22 @@
         whole = gram[0] + (cross + cross.T)
         blocks = jnp.concatenate([whole[:hc, :hc], whole[hc:, :hc], whole[hc:, hc:]], axis=0)
         g_part[it] = blocks.reshape(g_part.shape[1:])
-        peers(lambda j: scatter_copy(it, j, me, me).start())
-        g_parts[it, me] = g_part[it, me]
+        inside_half(lambda p: scatter_copy(it, p, place, place).start())
+        g_parts[it, place] = g_part[it, place]
         if it == 0:
             block_send(2)
-        peers(lambda j: scatter_copy(it, j, j, j).wait_recv())
-        g_sum[it] = jnp.sum(g_parts[it], axis=0)
-        peers(lambda j: gather_copy(it, j, me, me).start())
-        g_all[it, me] = g_sum[it]
+        inside_half(lambda p: scatter_copy(it, p, p, p).wait_recv())
+        g_half[it] = jnp.sum(g_parts[it], axis=0)
+        pair_copy(it).start()
         if it == 0:
             block_send(3)
-        peers(lambda j: gather_copy(it, j, j, j).wait_recv())
+        pair_copy(it).wait_recv()
+        g_sum[it] = g_half[it] + g_pair[it]
+        inside_half(lambda p: gather_copy(it, p, place, place).start())
+        g_all[it, place] = g_sum[it]
+        if it == 0:
+            block_send(4)
+        inside_half(lambda p: gather_copy(it, p, p, p).wait_recv())
 
         blocks = g_all[it].reshape(3 * hc, hc)
         top, corner, end = blocks[:hc], blocks[hc : 2 * hc], blocks[2 * hc :]
@@ -295,22 +320,27 @@
                 side_copy(it, 1, back_out, back_in, s, 1 - s).start()
 
         scale = core_weight * inverse
-        for w in range(0, wl, 2):
-            less = product(w, 2)
-            for i in range(2):
-                value = (matrix(0, w + i) - less[:, block(i)]) * scale
-                cube[:, w + i] = value.reshape(n, c_loc, rows)
-        for s in range(2):
-            @pl.when(has[s])
-            def _():
-                side_copy(it, 1, back_out, back_in, s, s).wait_recv()
-                start = 0 if s == 0 else rows - OV
-                inside = (lane >= start) & (lane < start + OV)
-                extra = back_in[it, s]
-                for w in range(wl):
-                    rolled = pltpu.roll(extra, (start - w * OV) % rows, 1)
-                    piece = jnp.where(inside, rolled * inverse, 0.0)
-                    cube[:, w] += piece.reshape(n, c_loc, rows)
+        step = 2 - cut % 2
+        for h, (first, count) in enumerate(halves):
+            for w in range(first, first + count, step):
+                less = product(w, step)
+                for i in range(step):
+                    value = (matrix(0, w + i) - less[:, block(i)]) * scale
+                    cube[:, w + i] = value.reshape(n, c_loc, rows)
+            for s in range(2):
+                @pl.when(has[s])
+                def _():
+                    if h == 0:
+                        side_copy(it, 1, back_out, back_in, s, s).wait_recv()
+                    start = 0 if s == 0 else rows - OV
+                    inside = (lane >= start) & (lane < start + OV)
+                    extra = back_in[it, s]
+                    for w in range(first, first + count):
+                        rolled = pltpu.roll(extra, (start - w * OV) % rows, 1)
+                        piece = jnp.where(inside, rolled * inverse, 0.0)
+                        cube[:, w] += piece.reshape(n, c_loc, rows)
+            if it == ITERS - 1:
+                peers(lambda j: final_copy(h, j, me, me).start())
 
         if it < ITERS - 1:
             def move(w):
@@ -319,43 +349,48 @@
                 recv[0, :, w] = value
                 put(w, value.reshape(total, rows))
 
-            if it == 0:
-                block_wait(1)
-                block_wait(2)
-            for w in range(cut):
-                move(w)
-            add_gram(0, cut, True)
-            if it == 0:
-                block_wait(3)
-            for w in range(cut, wl):
-                move(w)
-
-    peers(lambda j: final_copy(j, out.at[me], me).start())
+            for h, (first, count) in enumerate(halves):
+                if it == 0:
+                    block_wait(1 + h)
+                    block_wait(3 + h)
+                for w in range(first, first + count):
+                    move(w)
+                if h == 0:
+                    add_gram(first, count, True)
+
     out[me] = cube[me]
 
     def drain(j):
         for q in range(len(sets)):
             block_copy(q, j, me, me).wait_send()
+
+    def drain_half(p):
         for it in range(ITERS):
-            scatter_copy(it, j, me, me).wait_send()
-            gather_copy(it, j, me, me).wait_send()
+            scatter_copy(it, p, place, place).wait_send()
+            gather_copy(it, p, place, place).wait_send()
 
     peers(drain)
+    inside_half(drain_half)
+    for it in range(ITERS):
+        pair_copy(it).wait_send()
     for s in range(2):
         @pl.when(has[s])
         def _():
             for it in range(ITERS):
                 side_copy(it, 0, halo_out, halo_in, s, 1 - s).wait_send()
                 side_copy(it, 1, back_out, back_in, s, 1 - s).wait_send()
-    peers(lambda j: final_copy(j, out.at[j], j).wait_recv())
-    peers(lambda j: final_copy(j, out.at[me], me).wait_send())
+    for h in range(2):
+        peers(lambda j: final_copy(h, j, j, j).wait_recv())
+    for h in range(2):
+        peers(lambda j: final_copy(h, j, me, me).wait_send())
 
 
 def per_device(n, facets, estimate, dirty, weights, margin, blend_table, tau_steps):
     c_loc, width, rows = estimate.shape
     wl = width // n
     total = n * c_loc
-    piece = 3 * total // (2 * n)
+    half = n // 2
+    piece = 3 * total // n
     cut = lambda a: a.reshape(c_loc, n, wl, rows)
     vmem = pl.BlockSpec(memory_space=pltpu.VMEM)
     hbm = pl.BlockSpec(memory_space=pltpu.HBM)
@@ -376,25 +411,29 @@
             pltpu.VMEM((total, (wl + 2) * rows), BF16),
             pltpu.VMEM((total, (wl + 2) * rows), BF16),
             pltpu.VMEM((2, total, total), F32),
-            pltpu.VMEM((ITERS, n, piece, total // 2), F32),
-            pltpu.VMEM((ITERS, n, piece, total // 2), F32),
+            pltpu.VMEM((ITERS, half, piece, total // 2), F32),
+            pltpu.VMEM((ITERS, half, piece, total // 2), F32),
             pltpu.VMEM((ITERS, piece, total // 2), F32),
-            pltpu.VMEM((ITERS, n, piece, total // 2), F32),
+            pltpu.VMEM((ITERS, piece, total // 2), F32),
+            pltpu.VMEM((ITERS, piece, total // 2), F32),
+            pltpu.VMEM((ITERS, half, piece, total // 2), F32),
             pltpu.VMEM((ITERS, 2, total, rows), F32),
             pltpu.VMEM((ITERS, 2, total, rows), F32),
             pltpu.VMEM((2, total, rows), F32),
             pltpu.VMEM((ITERS, 2, total, rows), F32),
             pltpu.VMEM((ITERS, 2, total, rows), F32),
             dma((3,)),
-            dma((5, n)),
-            dma((5, n)),
-            dma((ITERS, 2, n)),
-            dma((ITERS, 2, n)),
+            dma((7, n)),
+            dma((7, n)),
+            dma((ITERS, 2, half)),
+            dma((ITERS, 2, half)),
+            dma((ITERS,)),
+            dma((ITERS,)),
             dma((ITERS, 2, 2)),
             dma((ITERS, 2, 2)),
         ],
         compiler_params=pltpu.CompilerParams(
-            collective_id=0, has_side_effects=True, vmem_limit_bytes=48 * 1024 * 1024
+            collective_id=0, has_side_effects=True, vmem_limit_bytes=127 * 1024 * 1024 // 2
         ),
         cost_estimate=pl.CostEstimate(
             flops=ITERS * 4 * total * total * wl * (rows + 2 * OV),

time: 137 us -> 126 us (0.920)
  Pallas kernels: 131 us -> 124 us
  local copies, waits for them, and re-layouts: 5.65 us -> 2.53 us
    pallas_call x1, Pallas kernels: 131 us -> 124 us  [per_device(): pl.pallas_call(functools.partial(kernel, n, facets), out_shape=jax.ShapeD...]
    unnamed x12 -> x0, local copies, waits for them, and re-layouts: 4.36 us -> none
where the time goes in v3:
time: 126 us
  Pallas kernels  124 us (98%)
  local copies, waits for them, and re-layouts  2.53 us (2%)
    pallas_call x1, Pallas kernels, per_device(): pl.pallas_call(functools.partial(kernel, n, facets), out_shape=jax.ShapeD...  124 us
    reshape x1, local copies, waits for them, and re-layouts, per_device(): return result.transpose(2, 0, 1, 3).reshape(c_loc, width, rows)  2.53 us

profile of v3, /device:TPU:0, one launch (start us, length us, event | category | flops | bytes accessed | tf_op | source)
XLA Modules:
  0.0 126.2 jit_solution(16057594261446779829)
XLA Ops:
  0.0 123.6 %denoise.1 = f32[16,8,16,128]{3,2,1,0:T(8,128)} custom-call(f32[16,16,8,128]{3,2,1,0:T(8,128)} %bitcast.7, f32[16,16,8,128]{3,2,1,0:T(8,128)} %bitcast.8, f32[16,16,8,128]{3,2,1,0:T(8,128)} %bitcast.9, s32[2]{0:T(128)} %margin.1, s32[2,160]{1,0:T(2,128)} %table.1, s32[2]{0:T(128)} %tau.1), custom_call_target="tpu_custom_call" | custom-call | flops 671088640 | bytes 4194304 | tf_op jit(solution)/shard_map/denoise/pallas_call | solution.py:399
  123.6 2.5 %copy.7 = f32[16,128,128]{2,1,0:T(8,128)} copy(f32[16,128,128]{2,0,1:T(8,128)} %bitcast.6) | data formatting | bytes 2097152 | tf_op jit(solution)/shard_map/reshape | solution.py:445

commit v4 on v3

--- a/solution.py
+++ b/solution.py
@@ -86,9 +86,12 @@
     for load in loads:
         load.wait()
 
-    cut = wl // 2
-    halves = ((0, cut), (cut, wl - cut))
-    sets = ((0, 0, wl),) + tuple((k, *h) for k in (1, 2) for h in halves)
+    part = max(1, wl // 4)
+    tail = wl - part
+    pieces = ((0, tail), (tail, part))
+    final_pieces = ((0, part), (part, tail))
+    dirty_pieces = [c for c in ((0, part), (part, tail - part), (tail, part)) if c[1] > 0]
+    sets = [(0, 0, wl)] + [(1, *c) for c in pieces] + [(2, *c) for c in dirty_pieces]
 
     def block_copy(q, j, origin, sem_at):
         k, first, count = sets[q]
@@ -232,12 +235,12 @@
         )
 
     def final_copy(h, j, origin, sem_at):
-        first, count = halves[h]
+        first, count = final_pieces[h]
         return pltpu.make_async_remote_copy(
             src_ref=cube.at[j, pl.ds(first, count)],
             dst_ref=out.at[origin, pl.ds(first, count)],
-            send_sem=send_sem.at[5 + h, j],
-            recv_sem=recv_sem.at[5 + h, sem_at],
+            send_sem=send_sem.at[len(sets) + h, j],
+            recv_sem=recv_sem.at[len(sets) + h, sem_at],
             device_id={"chan": j},
             device_id_type=MESH,
         )
@@ -261,7 +264,7 @@
                 put(w, matrix(0, w))
             add_gram(0, wl, True)
         else:
-            add_gram(cut, wl - cut, False)
+            add_gram(tail, part, False)
         for s in range(2):
             @pl.when(has[s])
             def _():
@@ -289,7 +292,8 @@
         inside_half(lambda p: gather_copy(it, p, place, place).start())
         g_all[it, place] = g_sum[it]
         if it == 0:
-            block_send(4)
+            for q in range(4, len(sets)):
+                block_send(q)
         inside_half(lambda p: gather_copy(it, p, p, p).wait_recv())
 
         blocks = g_all[it].reshape(3 * hc, hc)
@@ -320,8 +324,8 @@
                 side_copy(it, 1, back_out, back_in, s, 1 - s).start()
 
         scale = core_weight * inverse
-        step = 2 - cut % 2
-        for h, (first, count) in enumerate(halves):
+        step = 2 - part % 2
+        for h, (first, count) in enumerate(final_pieces):
             for w in range(first, first + count, step):
                 less = product(w, step)
                 for i in range(step):
@@ -349,16 +353,18 @@
                 recv[0, :, w] = value
                 put(w, value.reshape(total, rows))
 
-            for h, (first, count) in enumerate(halves):
+            for h, (first, count) in enumerate(pieces):
                 if it == 0:
                     block_wait(1 + h)
-                    block_wait(3 + h)
+                    for q in range(3, len(sets) - 1) if h == 0 else (len(sets) - 1,):
+                        block_wait(q)
                 for w in range(first, first + count):
                     move(w)
                 if h == 0:
                     add_gram(first, count, True)
 
-    out[me] = cube[me]
+    own = pltpu.make_async_copy(cube.at[me], out.at[me], in_sem.at[3])
+    own.start()
 
     def drain(j):
         for q in range(len(sets)):
@@ -379,6 +385,7 @@
             for it in range(ITERS):
                 side_copy(it, 0, halo_out, halo_in, s, 1 - s).wait_send()
                 side_copy(it, 1, back_out, back_in, s, 1 - s).wait_send()
+    own.wait()
     for h in range(2):
         peers(lambda j: final_copy(h, j, j, j).wait_recv())
     for h in range(2):
@@ -400,7 +407,7 @@
         functools.partial(kernel, n, facets),
         out_shape=jax.ShapeDtypeStruct((n, wl, c_loc, rows), F32),
         in_specs=[hbm, hbm, hbm, smem, vmem, smem],
-        out_specs=vmem,
+        out_specs=hbm,
         scratch_shapes=[
             pltpu.VMEM((c_loc, n, wl, rows), F32),
             pltpu.VMEM((c_loc, n, wl, rows), F32),
@@ -422,9 +429,9 @@
             pltpu.VMEM((2, total, rows), F32),
             pltpu.VMEM((ITERS, 2, total, rows), F32),
             pltpu.VMEM((ITERS, 2, total, rows), F32),
-            dma((3,)),
-            dma((7, n)),
-            dma((7, n)),
+            dma((4,)),
+            dma((8, n)),
+            dma((8, n)),
             dma((ITERS, 2, half)),
             dma((ITERS, 2, half)),
             dma((ITERS,)),

time: 126 us -> 125 us (level)
  Pallas kernels: 124 us -> 122 us
    pallas_call x1, Pallas kernels: 124 us -> 122 us  [per_device(): pl.pallas_call(functools.partial(kernel, n, facets), out_shape=jax.ShapeD...]
where the time goes in v4:
time: 125 us
  Pallas kernels  122 us (98%)
  local copies, waits for them, and re-layouts  2.53 us (2%)
    pallas_call x1, Pallas kernels, per_device(): pl.pallas_call(functools.partial(kernel, n, facets), out_shape=jax.ShapeD...  122 us
    reshape x1, local copies, waits for them, and re-layouts, per_device(): return result.transpose(2, 0, 1, 3).reshape(c_loc, width, rows)  2.53 us

profile of v4, /device:TPU:0, one launch (start us, length us, event | category | flops | bytes accessed | tf_op | source)
XLA Modules:
  0.0 124.9 jit_solution(4227211374717428041)
XLA Ops:
  0.0 122.3 %denoise.1 = f32[16,8,16,128]{3,2,1,0:T(8,128)} custom-call(f32[16,16,8,128]{3,2,1,0:T(8,128)} %bitcast.7, f32[16,16,8,128]{3,2,1,0:T(8,128)} %bitcast.8, f32[16,16,8,128]{3,2,1,0:T(8,128)} %bitcast.9, s32[2]{0:T(128)} %margin.1, s32[2,160]{1,0:T(2,128)} %table.1, s32[2]{0:T(128)} %tau.1), custom_call_target="tpu_custom_call" | custom-call | flops 671088640 | bytes 4194304 | tf_op jit(solution)/shard_map/denoise/pallas_call | solution.py:406
  122.3 2.5 %copy.7 = f32[16,128,128]{2,1,0:T(8,128)} copy(f32[16,128,128]{2,0,1:T(8,128)} %bitcast.6) | data formatting | bytes 2097152 | tf_op jit(solution)/shard_map/reshape | solution.py:452
